TPU v7x, 32 devices: a whole 2x2x4 slice. The times are simulated.
32 devices in a mesh: space: 8 (over z, x), snap: 4 (over y, core).
Axes of the slice: x: 2, y: 2, z: 4, core: 2. Of those that a mesh axis runs over, the one named last changes fastest.
Arguments:
- velocity: bfloat16 [512, 3, 8, 8, 128], P('snap', None, 'space')
- metric: float32 [9, 8, 8, 128], P(None, 'space'), may hold values from -4 to 4
- volume: float32 [8, 8, 128], P('space'), may hold values from 3.6621095e-05 to 0.00036621094
- blade_mask: int32 [8, 8], P('space'), may hold values 0 or 1
Outputs:
- gram: float32 [512, 512], P('snap', 'space')
All inputs are finite; a program needn't handle non-finite values. No bound on the sum of `blade_mask` on one device may be relied on, other than what follows from the above.
Results may differ from a plain program's by a relative error of at most 0.0003.
Values may be sent and summed in bfloat16 or wider, within the bound.
A program may use at most 64 MiB of HBM per device.

v0:
```python
import jax
import jax.numpy as jnp
from jax import lax
from jax.sharding import PartitionSpec as P


def with_halo(cells, sides, width):
    for axis, dim in sides:
        count = lax.axis_size(axis)
        head = lax.slice_in_dim(cells, 0, width, axis=dim)
        tail = lax.slice_in_dim(cells, cells.shape[dim] - width, cells.shape[dim], axis=dim)
        cells = jnp.concatenate(
            [
                lax.ppermute(tail, axis, [(i, (i + 1) % count) for i in range(count)]),
                cells,
                lax.ppermute(head, axis, [((i + 1) % count, i) for i in range(count)]),
            ],
            axis=dim,
        )
    return cells


def vorticity_scaled(padded, metric, weight):
    field = padded.astype(jnp.float32)
    core = field[:, :, 1:-1]
    d_i = (field[:, :, 2:] - field[:, :, :-2]) * 0.5
    pad_j = jnp.pad(core, ((0, 0), (0, 0), (0, 0), (1, 1), (0, 0)))
    d_j = (pad_j[:, :, :, 2:, :] - pad_j[:, :, :, :-2, :]) * 0.5
    pad_k = jnp.pad(core, ((0, 0), (0, 0), (0, 0), (0, 0), (1, 1)))
    d_k = (pad_k[:, :, :, :, 2:] - pad_k[:, :, :, :, :-2]) * 0.5

    def deriv(comp, axis_a):
        return (
            metric[3 * axis_a] * d_i[:, comp]
            + metric[3 * axis_a + 1] * d_j[:, comp]
            + metric[3 * axis_a + 2] * d_k[:, comp]
        )

    omega_x = deriv(2, 1) - deriv(1, 2)
    omega_y = deriv(0, 2) - deriv(2, 0)
    omega_z = deriv(1, 0) - deriv(0, 1)
    vort = jnp.stack([omega_x, omega_y, omega_z], axis=1)
    return (vort * weight).astype(jnp.bfloat16)


def shards(velocity, metric, volume, blade_mask):
    local_snaps = velocity.shape[0]
    padded = with_halo(velocity, (("space", 2),), 1)
    weight = jnp.sqrt(volume * blade_mask.astype(jnp.float32)[:, :, None])
    scaled = vorticity_scaled(padded, metric, weight)
    flat = scaled.reshape(local_snaps, -1)
    contract = (((1,), (1,)), ((), ()))
    block = lax.dot_general(
        flat,
        lax.all_gather(flat, "snap", axis=0, tiled=True),
        contract,
        preferred_element_type=jnp.float32,
    )
    return lax.psum_scatter(block, "space", scatter_dimension=1, tiled=True)


def solution(mesh):
    in_specs = (
        P("snap", None, "space", None, None),
        P(None, "space", None, None),
        P("space", None, None),
        P("space", None),
    )
    out_specs = P("snap", "space")
    return jax.shard_map(shards, mesh=mesh, in_specs=in_specs, out_specs=out_specs, check_vma=False)
```

profile of v0, /device:TPU:0, one launch (start us, length us, event | category | flops | bytes accessed | tf_op | source)
XLA Modules:
  0.0 152.2 jit_solution(7007297598796082790)
XLA Ops:
  6.5 0.0 all-gather.2.cloned.1.call-start
  6.5 6.0 %collective-permute-start.1 = (bf16[128,3,1,8,128]{4,3,2,1,0:T(8,128)(2,1)}, bf16[128,3,1,8,128]{4,3,2,1,0:T(8,128)(2,1)S(1)}, u32[]{:S(2)}, u32[]{:S(2)}) collective-permute-start(bf16[128,3,1,8,128]{4,3,2,1,0:T(8,128)(2,1)} %param.4), channel_id=1, source_target_pairs={{4,0},{8,4},{12,8},{16,12},{20,16},{24,20},{28,24},{0,28},{5,1},{9... | collective-permute-start | bytes 2359304 | tf_op jit(solution)/shard_map/ppermute | solution.py:16
  12.5 0.0 collective-permute-start
  12.5 0.7 convert_bitcast_fusion
  13.2 0.8 sqrt_bitcast_fusion
  13.9 0.8 slice_bitcast_fusion.5
  14.8 29.3 %collective-permute-done.1 = bf16[128,3,1,8,128]{4,3,2,1,0:T(8,128)(2,1)S(1)} collective-permute-done((bf16[128,3,1,8,128]{4,3,2,1,0:T(8,128)(2,1)}, bf16[128,3,1,8,128]{4,3,2,1,0:T(8,128)(2,1)S(1)}, u32[]{:S(2)}, u32[]{:S(2)}) %collective-permute-start.1) | collective-permute-done | bytes 786464 | tf_op jit(solution)/shard_map/ppermute | solution.py:16
  44.1 0.3 collective-permute-done
  44.3 1.7 %maximum_convert_fusion = f32[128,3,3,8,128]{4,3,2,1,0:T(8,128)S(1)} fusion(bf16[128,3,1,8,128]{4,3,2,1,0:T(8,128)(2,1)S(1)} %collective-permute-done.1, bf16[128,3,1,8,128]{4,3,2,1,0:T(8,128)(2,1)} %param.4, bf16[128,3,1,8,128]{4,3,2,1,0:T(8,128)(2,1)S(1)} %collective-permute-done), kind=kLoop, calls=%fused_computation.4 | loop fusion | flops 3538944 | bytes 7077888 | tf_op jit(solution)/shard_map/convert_element_type | solution.py:24
  46.1 0.3 fusion.5
  46.4 1.1 fusion.1
  47.5 0.2 add_subtract_fusion
  47.7 0.2 add_subtract_fusion.1
  47.9 0.2 add_subtract_fusion.2
  48.1 0.1 pad_maximum_fusion
  48.2 1.1 fusion.4
  49.3 0.0 all-gather.2.cloned.1.call-update
  49.4 0.0 reduce-scatter.2.cloned.1.call-start
  49.4 30.1 %all-gather.2.cloned.1.call-done = bf16[512,3072]{1,0:T(8,128)(2,1)} async-done(((bf16[128,3072]{1,0:T(8,128)(2,1)}), bf16[512,3072]{1,0:T(8,128)(2,1)}) %all-gather.2.cloned.1.call-update) | async-done | bytes 3145744 | tf_op jit(solution)/shard_map/all_gather | solution.py:55
  79.5 3.8 %fusion.6 = f32[128,512]{0,1:T(8,128)} fusion(bf16[128,3072]{1,0:T(8,128)(2,1)} %fusion.4, bf16[512,3072]{1,0:T(8,128)(2,1)} %all-gather.2.cloned.1.call-done), kind=kOutput, calls=%fused_computation.29 | convolution fusion | flops 402653184 | bytes 4194304 | tf_op jit(solution)/shard_map/dot_general | solution.py:53
  83.4 0.0 reduce-scatter.2.cloned.1.call-update
  83.4 61.9 %reduce-scatter.2.cloned.1.call-done = f32[128,64]{0,1:T(8,128)} async-done(((f32[128,512]{0,1:T(8,128)}), f32[128,64]{0,1:T(8,128)}) %reduce-scatter.2.cloned.1.call-update) | async-done | bytes 32784 | tf_op jit(solution)/shard_map/reduce_scatter | solution.py:59
  (1 shorter events, 0.0 us)
Async XLA Ops:
  6.5 73.0 %all-gather.2.cloned.1.call-start = ((), (), s32[]{:S(2)}) async-start(), calls=%async_computation.1 | async-start | bytes 3932160 | tf_op jit(solution)/shard_map/all_gather | solution.py:55
  6.5 37.5 %collective-permute-start.1 = (bf16[128,3,1,8,128]{4,3,2,1,0:T(8,128)(2,1)}, bf16[128,3,1,8,128]{4,3,2,1,0:T(8,128)(2,1)S(1)}, u32[]{:S(2)}, u32[]{:S(2)}) collective-permute-start(bf16[128,3,1,8,128]{4,3,2,1,0:T(8,128)(2,1)} %param.4), channel_id=1, source_target_pairs={{4,0},{8,4},{12,8},{16,12},{20,16},{24,20},{28,24},{0,28},{5,1},{9... | collective-permute-start | bytes 2359304 | tf_op jit(solution)/shard_map/ppermute | solution.py:16
  12.5 31.8 %collective-permute-start = (bf16[128,3,1,8,128]{4,3,2,1,0:T(8,128)(2,1)}, bf16[128,3,1,8,128]{4,3,2,1,0:T(8,128)(2,1)S(1)}, u32[]{:S(2)}, u32[]{:S(2)}) collective-permute-start(bf16[128,3,1,8,128]{4,3,2,1,0:T(8,128)(2,1)} %param.4), channel_id=1, source_target_pairs={{0,4},{4,8},{8,12},{12,16},{16,20},{20,24},{24,28},{28,0},{1,5},{5... | collective-permute-start | bytes 2359304 | tf_op jit(solution)/shard_map/ppermute | solution.py:14
  49.4 96.0 %reduce-scatter.2.cloned.1.call-start = ((), (), s32[]{:S(2)}) async-start(), calls=%async_computation.2 | async-start | bytes 294912 | tf_op jit(solution)/shard_map/reduce_scatter | solution.py:59
Sparse Core Ops, SparseCore 0:
  49.5 30.0 all-gather.1
  83.5 61.7 reduce-scatter.1
where the time goes:
time: 152 us
  waiting for transfers between devices  122 us (80%)
  between operations  13.4 us (9%)
  other arithmetic  6.37 us (4%)
  starting transfers between devices  6.02 us (4%)
  matrix products  3.81 us (3%)
    reduce_scatter x1, waiting for transfers between devices, shards(): return lax.psum_scatter(block, 'space', scatter_dimension=1, tiled=True)  61.9 us
    all_gather x1, waiting for transfers between devices, shards(): lax.all_gather(flat, 'snap', axis=0, tiled=True)  30.1 us
    ppermute x1, waiting for transfers between devices, with_halo(): lax.ppermute(head, axis, [((i + 1) % count, i) for i in range(count)])  29.3 us
    ppermute x1, starting transfers between devices, with_halo(): lax.ppermute(head, axis, [((i + 1) % count, i) for i in range(count)])  5.98 us
    dot_general x1, matrix products, shards(): lax.dot_general(flat, lax.all_gather(flat, 'snap', axis=0, tiled=True), c...  3.81 us
  transfers between devices with their start and end apart: 4, of which 4 were waited for; matrix products, arithmetic and copies ran while one was open for 1% of the time, Pallas kernels for 0%

commit v1 on v0

v1 whole, which is shorter than its diff:
```python
import functools

import jax
import jax.numpy as jnp
from jax import lax
from jax.experimental import pallas as pl
from jax.experimental.pallas import tpu as pltpu
from jax.sharding import PartitionSpec as P

ROWS = 16


def remote(src, dst, send_sem, recv_sem, **where):
    return pltpu.make_async_remote_copy(
        src_ref=src,
        dst_ref=dst,
        send_sem=send_sem,
        recv_sem=recv_sem,
        device_id=where,
        device_id_type=pl.DeviceIdType.MESH,
    )


def kernel(
    n_space, n_snap, u_ref, coef_ref, out_ref,
    side, far, gathered, partial, landed,
    x_s, x_r, z_s, z_r, m_s, m_r, y_s, y_r, f_s, f_r, r_s, r_r,
):
    snaps, width = u_ref.shape
    cells = width // 3
    chunks = snaps // ROWS
    cols = landed.shape[1]
    per_dev = snaps // cols
    chips = n_snap // 2

    i = lax.axis_index("space")
    s = lax.axis_index("snap")
    odd = lax.rem(i, 2)
    core = lax.rem(s, 2)
    chip = s // 2
    partner = i + 1 - 2 * odd
    ahead = lax.rem(i + 2 - 4 * odd + n_space, n_space)
    mate = s + 1 - 2 * core

    def peer(o):
        return 2 * lax.rem(chip + o, chips) + core

    def origin(o):
        return 2 * lax.rem(chip + chips - o, chips) + core

    barrier = pltpu.get_barrier_semaphore()

    def greet(d, carry):
        pl.semaphore_signal(
            barrier, inc=1, device_id={"space": lax.rem(i + d, n_space)},
            device_id_type=pl.DeviceIdType.MESH,
        )
        return carry

    lax.fori_loop(1, n_space, greet, 0)
    pl.semaphore_signal(
        barrier, inc=1, device_id={"snap": mate}, device_id_type=pl.DeviceIdType.MESH
    )
    for o in range(1, chips):
        pl.semaphore_signal(
            barrier, inc=1, device_id={"snap": peer(o)}, device_id_type=pl.DeviceIdType.MESH
        )
    pl.semaphore_wait(barrier, n_space - 1 + chips)

    def rows(t):
        return pl.ds(pl.multiple_of(t * ROWS, ROWS), ROWS)

    def x_copy(t):
        return remote(u_ref.at[rows(t)], side.at[rows(t)], x_s.at[t], x_r.at[t], space=partner)

    def z_copy(t):
        return remote(side.at[rows(t)], far.at[rows(t)], z_s.at[t], z_r.at[t], space=ahead)

    def m_copy(t):
        block = gathered.at[s, rows(t)]
        return remote(block, block, m_s.at[t], m_r.at[t], snap=mate)

    def y_copy(o, t):
        block = gathered.at[s, rows(t)]
        return remote(block, block, y_s.at[o - 1, t], y_r.at[o - 1, t], snap=peer(o))

    def f_copy(o, t):
        block = gathered.at[origin(o), rows(t)]
        return remote(block, block, f_s.at[o - 1, t], f_r.at[o - 1, t], snap=mate)

    def y_arrival(o, t):
        block = gathered.at[origin(o), rows(t)]
        return remote(block, block, y_s.at[o - 1, t], y_r.at[o - 1, t], snap=peer(o))

    def m_arrival(t):
        block = gathered.at[mate, rows(t)]
        return remote(block, block, m_s.at[t], m_r.at[t], snap=mate)

    def f_origin(o):
        return 2 * lax.rem(chip + chips - o, chips) + 1 - core

    def f_arrival(o, t):
        block = gathered.at[f_origin(o), rows(t)]
        return remote(block, block, f_s.at[o - 1, t], f_r.at[o - 1, t], snap=mate)

    lane = lax.rem(lax.broadcasted_iota(jnp.int32, (ROWS, cells), 1), 128)
    sign = (1 - 2 * odd).astype(jnp.float32)

    def vorticity(t):
        d_i, d_j, d_k = [], [], []
        for c in range(3):
            part = pl.ds(c * cells, cells)
            here = u_ref[rows(t), part].astype(jnp.float32)
            near = side[rows(t), part].astype(jnp.float32)
            away = far[rows(t), part].astype(jnp.float32)
            d_i.append((near - away) * sign)
            edge = jnp.zeros((ROWS, 128), jnp.float32)
            d_j.append(
                jnp.concatenate([here[:, 128:], edge], axis=1)
                - jnp.concatenate([edge, here[:, :-128]], axis=1)
            )
            d_k.append(
                jnp.where(lane == 127, 0.0, pltpu.roll(here, cells - 1, 1))
                - jnp.where(lane == 0, 0.0, pltpu.roll(here, 1, 1))
            )

        def deriv(comp, a):
            return (
                coef_ref[pl.ds(3 * a, 1), :] * d_i[comp]
                + coef_ref[pl.ds(3 * a + 1, 1), :] * d_j[comp]
                + coef_ref[pl.ds(3 * a + 2, 1), :] * d_k[comp]
            )

        for c, (p, q) in enumerate(((2, 1), (0, 2), (1, 0))):
            gathered[s, rows(t), pl.ds(c * cells, cells)] = (
                deriv(p, q) - deriv(q, p)
            ).astype(jnp.bfloat16)

    def launch(t, carry):
        x_copy(t).start()
        return carry

    lax.fori_loop(0, chunks, launch, 0)

    def step(t, carry):
        @pl.when(t < chunks)
        def _():
            x_copy(t).wait_recv()
            z_copy(t).start()

        @pl.when(jnp.logical_and(t >= 1, t < chunks + 1))
        def _():
            z_copy(t - 1).wait_recv()
            vorticity(t - 1)
            for o in range(1, chips):
                y_copy(o, t - 1).start()
            m_copy(t - 1).start()

        @pl.when(t >= 3)
        def _():
            for o in range(1, chips):
                y_arrival(o, t - 3).wait_recv()
                f_copy(o, t - 3).start()

        return carry

    def r_copy(block):
        return remote(
            partial.at[block], landed.at[i], r_s.at[block], r_r.at[i], space=block
        )

    def r_arrival(source):
        return remote(
            partial.at[i], landed.at[source], r_s.at[source], r_r.at[source], space=source
        )

    def product(dev):
        own = gathered[s]
        for h in range(per_dev):
            block = dev * per_dev + h
            partial[block] = lax.dot_general(
                gathered[dev, pl.ds(h * cols, cols), :], own, (((1,), (1,)), ((), ())),
                preferred_element_type=jnp.float32,
            )

            @pl.when(block != i)
            def _():
                r_copy(block).start()

    lax.fori_loop(0, chunks + 1, step, 0)
    product(s)
    lax.fori_loop(chunks + 1, chunks + 3, step, 0)

    def await_m(t, carry):
        m_arrival(t).wait_recv()
        return carry

    lax.fori_loop(0, chunks, await_m, 0)
    product(mate)
    for o in range(1, chips):
        product(origin(o))
    for o in range(1, chips):
        def await_f(t, carry):
            f_arrival(o, t).wait_recv()
            return carry

        lax.fori_loop(0, chunks, await_f, 0)
        product(f_origin(o))

    def add(d, total):
        source = lax.rem(i + d, n_space)
        r_arrival(source).wait_recv()
        return total + landed[source]

    total = lax.fori_loop(1, n_space, add, partial[i])
    out_ref[...] = total

    def drain(t, carry):
        x_copy(t).wait_send()
        z_copy(t).wait_send()
        m_copy(t).wait_send()
        for o in range(1, chips):
            y_copy(o, t).wait_send()
            f_copy(o, t).wait_send()
        return carry

    lax.fori_loop(0, chunks, drain, 0)

    def drain_r(d, carry):
        r_copy(lax.rem(i + d, n_space)).wait_send()
        return carry

    lax.fori_loop(1, n_space, drain_r, 0)


def shards(n_space, n_snap, velocity, metric, volume, blade_mask):
    snaps = velocity.shape[0]
    u = velocity.reshape(snaps, -1)
    width = u.shape[1]
    weight = 0.5 * jnp.sqrt(volume * blade_mask.astype(jnp.float32)[:, :, None])
    coef = (metric * weight).reshape(9, -1)
    cols = snaps * n_snap // n_space
    chunks = snaps // ROWS
    chips = n_snap // 2
    far = max(chips - 1, 1)
    dma = pltpu.SemaphoreType.DMA
    return pl.pallas_call(
        functools.partial(kernel, n_space, n_snap),
        out_shape=jax.ShapeDtypeStruct((cols, snaps), jnp.float32),
        in_specs=[pl.BlockSpec(memory_space=pltpu.VMEM)] * 2,
        out_specs=pl.BlockSpec(memory_space=pltpu.VMEM),
        scratch_shapes=[
            pltpu.VMEM((snaps, width), jnp.bfloat16),
            pltpu.VMEM((snaps, width), jnp.bfloat16),
            pltpu.VMEM((n_snap, snaps, width), jnp.bfloat16),
            pltpu.VMEM((n_space, cols, snaps), jnp.float32),
            pltpu.VMEM((n_space, cols, snaps), jnp.float32),
            dma((chunks,)), dma((chunks,)), dma((chunks,)), dma((chunks,)),
            dma((chunks,)), dma((chunks,)),
            dma((far, chunks)), dma((far, chunks)), dma((far, chunks)), dma((far, chunks)),
            dma((n_space,)), dma((n_space,)),
        ],
        compiler_params=pltpu.CompilerParams(
            collective_id=0, has_side_effects=True, vmem_limit_bytes=48 * 1024 * 1024
        ),
    )(u, coef).T


def solution(mesh):
    in_specs = (
        P("snap", None, "space", None, None),
        P(None, "space", None, None),
        P("space", None, None),
        P("space", None),
    )
    body = functools.partial(shards, mesh.shape["space"], mesh.shape["snap"])
    return jax.shard_map(body, mesh=mesh, in_specs=in_specs, out_specs=P("snap", "space"), check_vma=False)
```

time: 152 us -> 45.5 us (0.30)
  the two profiles are of different devices: /device:TPU:0 before, /device:TPU:7 now
where the time goes in v1:
time: 45.5 us; the launch traced here: 45.2 us
  Pallas kernels  41.1 us (90%)
  local copies, waits for them, and re-layouts  2.58 us (6%)
  other arithmetic  1.54 us (3%)
    pallas_call x1, Pallas kernels, shards(): pl.pallas_call(functools.partial(kernel, n_space, n_snap), out_shape=jax....  41.1 us
    unnamed x6, local copies, waits for them, and re-layouts  2.58 us

profile of v1, /device:TPU:7, one launch (start us, length us, event | category | flops | bytes accessed | tf_op | source)
XLA Modules:
  0.0 45.2 jit_solution(7886343289360451019)
XLA Ops:
  0.0 0.0 copy-start
  0.0 0.7 %copy-done = s32[1,8]{1,0:T(1,128)S(1)} copy-done((s32[1,8]{1,0:T(1,128)S(1)}, s32[1,8]{1,0:T(1,128)}, u32[]{:S(2)}) %copy-start) | copy-done | bytes 56
  0.7 0.8 %multiply_bitcast_fusion.1 = f32[8,128]{1,0:T(8,128)S(1)} fusion(f32[1,8,128]{2,1,0:T(8,128)} %param.6, f32[8]{0:T(128)S(1)} %convert_bitcast_fusion), kind=kLoop, calls=%fused_computation.2 | loop fusion | flops 2048 | bytes 8224 | tf_op jit(solution)/shard_map/mul | solution.py:241
  1.4 0.8 %multiply_bitcast_fusion = f32[9,8,128]{2,1,0:T(8,128)S(1)} fusion(f32[9,1,8,128]{3,2,1,0:T(8,128)} %param.5, f32[8,128]{1,0:T(8,128)S(1)} %multiply_bitcast_fusion.1), kind=kLoop, calls=%fused_computation.1 | loop fusion | flops 9216 | bytes 77824
  2.2 1.3 %copy.8 = bf16[16,8,24,128]{3,1,2,0:T(8,128)(2,1)S(1)} copy(bf16[16,8,24,128]{3,2,1,0:T(8,128)(2,1)} %bitcast.18) | data formatting | bytes 1572864
  3.5 41.1 %shard_map.46 = f32[64,128]{1,0:T(8,128)S(1)} custom-call(bf16[128,3072]{1,0:T(8,128)(2,1)S(1)} %bitcast.15, f32[9,1024]{1,0:T(8,128)S(1)} %bitcast.16), custom_call_target="tpu_custom_call" | custom-call | tf_op jit(solution)/shard_map/pallas_call | solution.py:247
  44.6 0.6 %copy.10 = f32[128,64]{0,1:T(8,128)} copy(f32[128,64]{0,1:T(8,128)S(1)} %bitcast.17) | data formatting | bytes 65536
  (3 shorter events, 0.0 us)
Async XLA Ops:
  0.0 0.7 %copy-start = (s32[1,8]{1,0:T(1,128)S(1)}, s32[1,8]{1,0:T(1,128)}, u32[]{:S(2)}) copy-start(s32[1,8]{1,0:T(1,128)} %param.7) | copy-start | bytes 100

commit v2 on v1

v2 whole, which is shorter than its diff:
```python
import functools

import jax
import jax.numpy as jnp
from jax import lax
from jax.experimental import pallas as pl
from jax.experimental.pallas import tpu as pltpu
from jax.sharding import PartitionSpec as P

ROWS = 16


def remote(src, dst, send_sem, recv_sem, **where):
    return pltpu.make_async_remote_copy(
        src_ref=src,
        dst_ref=dst,
        send_sem=send_sem,
        recv_sem=recv_sem,
        device_id=where,
        device_id_type=pl.DeviceIdType.MESH,
    )


def kernel(
    n_space, n_snap, u_ref, metric_ref, volume_ref, mask_ref, out_ref,
    coef_ref, side, far, gathered, partial, landed,
    x_s, x_r, z_s, z_r, m_s, m_r, y_s, y_r, f_s, f_r, r_s, r_r,
):
    snaps, width = u_ref.shape
    cells = width // 3
    chunks = snaps // ROWS
    cols = landed.shape[1]
    per_dev = snaps // cols
    chips = n_snap // 2

    i = lax.axis_index("space")
    s = lax.axis_index("snap")
    odd = lax.rem(i, 2)
    core = lax.rem(s, 2)
    chip = s // 2
    partner = i + 1 - 2 * odd
    ahead = lax.rem(i + 2 - 4 * odd + n_space, n_space)
    mate = s + 1 - 2 * core

    def peer(o):
        return 2 * lax.rem(chip + o, chips) + core

    def origin(o):
        return 2 * lax.rem(chip + chips - o, chips) + core

    barrier = pltpu.get_barrier_semaphore()

    def greet(d, carry):
        pl.semaphore_signal(
            barrier, inc=1, device_id={"space": lax.rem(i + d, n_space)},
            device_id_type=pl.DeviceIdType.MESH,
        )
        return carry

    lax.fori_loop(1, n_space, greet, 0)
    pl.semaphore_signal(
        barrier, inc=1, device_id={"snap": mate}, device_id_type=pl.DeviceIdType.MESH
    )
    for o in range(1, chips):
        pl.semaphore_signal(
            barrier, inc=1, device_id={"snap": peer(o)}, device_id_type=pl.DeviceIdType.MESH
        )
    pl.semaphore_wait(barrier, n_space - 1 + chips)

    def rows(t):
        return pl.ds(pl.multiple_of(t * ROWS, ROWS), ROWS)

    def part(p):
        return pl.ds(p * cells, cells)

    def x_copy(t, p):
        where = (rows(t), part(p))
        return remote(u_ref.at[where], side.at[where], x_s.at[t, p], x_r.at[t, p], space=partner)

    def z_copy(t, p):
        block = (rows(t), part(p))
        return remote(side.at[block], far.at[block], z_s.at[t, p], z_r.at[t, p], space=ahead)

    def m_copy(t):
        block = gathered.at[s, rows(t)]
        return remote(block, block, m_s.at[t], m_r.at[t], snap=mate)

    def m_arrival(t):
        block = gathered.at[mate, rows(t)]
        return remote(block, block, m_s.at[t], m_r.at[t], snap=mate)

    def cross(source, o, t, p):
        block = gathered.at[source, rows(t), part(p)]
        return remote(block, block, y_s.at[o - 1, t, p], y_r.at[o - 1, t, p], snap=peer(o))

    def y_copy(o, t, p):
        return cross(s, o, t, p)

    def y_arrival(o, t, p):
        return cross(origin(o), o, t, p)

    def onward(source, o, t, p):
        block = gathered.at[source, rows(t), part(p)]
        return remote(block, block, f_s.at[o - 1, t, p], f_r.at[o - 1, t, p], snap=mate)

    def f_copy(o, t, p):
        return onward(origin(o), o, t, p)

    def f_origin(o):
        return 2 * lax.rem(chip + chips - o, chips) + 1 - core

    def f_arrival(o, t, p):
        return onward(f_origin(o), o, t, p)

    lane = lax.rem(lax.broadcasted_iota(jnp.int32, (ROWS, cells), 1), 128)
    sign = (1 - 2 * odd).astype(jnp.float32)

    def vorticity(t):
        d_i, d_j, d_k = [], [], []
        for c in range(3):
            here = u_ref[rows(t), part(c)].astype(jnp.float32)
            near = side[rows(t), part(c)].astype(jnp.float32)
            away = far[rows(t), part(c)].astype(jnp.float32)
            d_i.append((near - away) * sign)
            edge = jnp.zeros((ROWS, 128), jnp.float32)
            d_j.append(
                jnp.concatenate([here[:, 128:], edge], axis=1)
                - jnp.concatenate([edge, here[:, :-128]], axis=1)
            )
            d_k.append(
                jnp.where(lane == 127, 0.0, pltpu.roll(here, cells - 1, 1))
                - jnp.where(lane == 0, 0.0, pltpu.roll(here, 1, 1))
            )

        def deriv(comp, a):
            return (
                coef_ref[pl.ds(3 * a, 1), :] * d_i[comp]
                + coef_ref[pl.ds(3 * a + 1, 1), :] * d_j[comp]
                + coef_ref[pl.ds(3 * a + 2, 1), :] * d_k[comp]
            )

        for c, (p, q) in enumerate(((2, 1), (0, 2), (1, 0))):
            gathered[s, rows(t), part(c)] = (
                deriv(p, q) - deriv(q, p)
            ).astype(jnp.bfloat16)

    def launch(t, carry):
        for p in range(3):
            x_copy(t, p).start()
        return carry

    lax.fori_loop(0, chunks, launch, 0)

    for j in range(cells // 128):
        line = pl.ds(j, 1)
        weight = 0.5 * jnp.sqrt(volume_ref[line, :] * mask_ref[0, j].astype(jnp.float32))
        coef_ref[:, pl.ds(j * 128, 128)] = metric_ref[:, j, :] * weight

    def step(t, carry):
        @pl.when(t < chunks)
        def _():
            for p in range(3):
                x_copy(t, p).wait_recv()
                z_copy(t, p).start()

        @pl.when(jnp.logical_and(t >= 1, t < chunks + 1))
        def _():
            for p in range(3):
                z_copy(t - 1, p).wait_recv()
            vorticity(t - 1)
            for p in range(3):
                for o in range(1, chips):
                    y_copy(o, t - 1, p).start()
            m_copy(t - 1).start()

        @pl.when(t >= 3)
        def _():
            for p in range(3):
                for o in range(1, chips):
                    y_arrival(o, t - 3, p).wait_recv()
                    f_copy(o, t - 3, p).start()

        return carry

    def r_copy(block):
        return remote(
            partial.at[block], landed.at[i], r_s.at[block], r_r.at[i], space=block
        )

    def r_arrival(source):
        return remote(
            partial.at[i], landed.at[source], r_s.at[source], r_r.at[source], space=source
        )

    def product(dev, h):
        block = dev * per_dev + h
        partial[block] = lax.dot_general(
            gathered[dev, pl.ds(h * cols, cols), :], gathered[s], (((1,), (1,)), ((), ())),
            preferred_element_type=jnp.float32,
        )

        @pl.when(block != i)
        def _():
            r_copy(block).start()

    def await_m(t, carry):
        m_arrival(t).wait_recv()
        return carry

    per_block = cols // ROWS

    def product_f(o, h):
        def await_f(t, carry):
            for p in range(3):
                f_arrival(o, t, p).wait_recv()
            return carry

        lax.fori_loop(h * per_block, (h + 1) * per_block, await_f, 0)
        product(f_origin(o), h)

    lax.fori_loop(0, chunks + 1, step, 0)
    for h in range(per_dev):
        product(s, h)
    lax.fori_loop(0, chunks, await_m, 0)
    for h in range(per_dev):
        product(mate, h)
    lax.fori_loop(chunks + 1, chunks + 2, step, 0)
    for o in range(1, chips):
        for h in range(per_dev - 1):
            product(origin(o), h)
    lax.fori_loop(chunks + 2, chunks + 3, step, 0)
    for o in range(1, chips):
        for h in range(per_dev - 1):
            product_f(o, h)
    for o in range(1, chips):
        product(origin(o), per_dev - 1)
    for o in range(1, chips):
        product_f(o, per_dev - 1)

    def add(d, total):
        source = lax.rem(i + d, n_space)
        r_arrival(source).wait_recv()
        return total + landed[source]

    total = lax.fori_loop(1, n_space, add, partial[i])
    out_ref[...] = total

    def drain(t, carry):
        m_copy(t).wait_send()
        for p in range(3):
            x_copy(t, p).wait_send()
            z_copy(t, p).wait_send()
            for o in range(1, chips):
                y_copy(o, t, p).wait_send()
                f_copy(o, t, p).wait_send()
        return carry

    lax.fori_loop(0, chunks, drain, 0)

    def drain_r(d, carry):
        r_copy(lax.rem(i + d, n_space)).wait_send()
        return carry

    lax.fori_loop(1, n_space, drain_r, 0)


def shards(n_space, n_snap, velocity, metric, volume, blade_mask):
    snaps = velocity.shape[0]
    u = velocity.reshape(snaps, -1)
    width = u.shape[1]
    cols = snaps * n_snap // n_space
    chunks = snaps // ROWS
    chips = n_snap // 2
    far = max(chips - 1, 1)
    dma = pltpu.SemaphoreType.DMA
    return pl.pallas_call(
        functools.partial(kernel, n_space, n_snap),
        out_shape=jax.ShapeDtypeStruct((cols, snaps), jnp.float32),
        in_specs=[pl.BlockSpec(memory_space=pltpu.VMEM)] * 3
        + [pl.BlockSpec(memory_space=pltpu.SMEM)],
        out_specs=pl.BlockSpec(memory_space=pltpu.VMEM),
        scratch_shapes=[
            pltpu.VMEM((9, width // 3), jnp.float32),
            pltpu.VMEM((snaps, width), jnp.bfloat16),
            pltpu.VMEM((snaps, width), jnp.bfloat16),
            pltpu.VMEM((n_snap, snaps, width), jnp.bfloat16),
            pltpu.VMEM((n_space, cols, snaps), jnp.float32),
            pltpu.VMEM((n_space, cols, snaps), jnp.float32),
            dma((chunks, 3)), dma((chunks, 3)), dma((chunks, 3)), dma((chunks, 3)),
            dma((chunks,)), dma((chunks,)),
            dma((far, chunks, 3)), dma((far, chunks, 3)),
            dma((far, chunks, 3)), dma((far, chunks, 3)),
            dma((n_space,)), dma((n_space,)),
        ],
        compiler_params=pltpu.CompilerParams(
            collective_id=0, has_side_effects=True, vmem_limit_bytes=48 * 1024 * 1024
        ),
    )(u, metric[:, 0], volume[0], blade_mask).T


def solution(mesh):
    in_specs = (
        P("snap", None, "space", None, None),
        P(None, "space", None, None),
        P("space", None, None),
        P("space", None),
    )
    body = functools.partial(shards, mesh.shape["space"], mesh.shape["snap"])
    return jax.shard_map(body, mesh=mesh, in_specs=in_specs, out_specs=P("snap", "space"), check_vma=False)
```

time: 45.5 us -> 43.8 us (0.963)
  other arithmetic: 1.54 us -> 0 us
    unnamed x1 -> x0, other arithmetic: 0.78 us -> none
    mul x2 -> x0, other arithmetic: 0.76 us -> none  [the longest x1 0.76 us: shards(): coef = (metric * weight).reshape(9, -1)]
    unnamed x6 -> x8, local copies, waits for them, and re-layouts: 2.58 us -> 2.54 us
where the time goes in v2:
time: 43.8 us; the launch traced here: 43.6 us
  Pallas kernels  41.1 us (94%)
  local copies, waits for them, and re-layouts  2.54 us (6%)
    pallas_call x1, Pallas kernels, shards(): pl.pallas_call(functools.partial(kernel, n_space, n_snap), out_shape=jax....  41.1 us
    unnamed x8, local copies, waits for them, and re-layouts  2.54 us

profile of v2, /device:TPU:7, one launch (start us, length us, event | category | flops | bytes accessed | tf_op | source)
XLA Modules:
  0.0 43.6 jit_solution(10989806476215823173)
XLA Ops:
  0.0 0.0 copy-start
  0.0 0.0 copy-start.1
  0.0 1.3 %copy.7 = bf16[16,8,24,128]{3,1,2,0:T(8,128)(2,1)S(1)} copy(bf16[16,8,24,128]{3,2,1,0:T(8,128)(2,1)} %bitcast.12) | data formatting | bytes 1572864
  1.3 0.0 copy-start.2
  1.3 0.0 copy-done
  1.3 0.0 copy-done.1
  1.3 0.6 %copy-done.2 = s32[1,8]{1,0:T(1,128)S(1)} copy-done((s32[1,8]{1,0:T(1,128)S(1)}, s32[1,8]{1,0:T(1,128)}, u32[]{:S(2)}) %copy-start.2) | copy-done | bytes 56
  2.0 41.1 %shard_map.46 = f32[64,128]{1,0:T(8,128)S(1)} custom-call(bf16[128,3072]{1,0:T(8,128)(2,1)S(1)} %bitcast.8, f32[9,8,128]{2,1,0:T(8,128)S(1)} %bitcast.10, f32[8,128]{1,0:T(8,128)S(1)} %bitcast.11, s32[1,8]{1,0:T(1,128)S(1)} %copy-done.2), custom_call_target="tpu_custom_call" | custom-call | tf_op jit(solution)/shard_map/pallas_call | solution.py:276
  43.0 0.6 %copy.9 = f32[128,64]{0,1:T(8,128)} copy(f32[128,64]{0,1:T(8,128)S(1)} %bitcast.9) | data formatting | bytes 65536
Async XLA Ops:
  0.0 1.3 %copy-start = (f32[9,1,8,128]{3,2,1,0:T(8,128)S(1)}, f32[9,1,8,128]{3,2,1,0:T(8,128)}, u32[]{:S(2)}) copy-start(f32[9,1,8,128]{3,2,1,0:T(8,128)} %param.5) | copy-start | bytes 110596
  0.0 1.3 %copy-start.1 = (f32[1,8,128]{2,1,0:T(8,128)S(1)}, f32[1,8,128]{2,1,0:T(8,128)}, u32[]{:S(2)}) copy-start(f32[1,8,128]{2,1,0:T(8,128)} %param.6) | copy-start | bytes 12292
  1.3 0.7 %copy-start.2 = (s32[1,8]{1,0:T(1,128)S(1)}, s32[1,8]{1,0:T(1,128)}, u32[]{:S(2)}) copy-start(s32[1,8]{1,0:T(1,128)} %mask_ref.1) | copy-start | bytes 100

commit v3 on v2

--- a/solution.py
+++ b/solution.py
@@ -24,7 +24,7 @@
 def kernel(
     n_space, n_snap, u_ref, metric_ref, volume_ref, mask_ref, out_ref,
     coef_ref, side, far, gathered, partial, landed,
-    x_s, x_r, z_s, z_r, m_s, m_r, y_s, y_r, f_s, f_r, r_s, r_r,
+    x_s, x_r, z_s, z_r, m_s, m_r, y_s, y_r, f_s, f_r, r_s, r_r, ring, pair,
 ):
     snaps, width = u_ref.shape
     cells = width // 3
@@ -40,6 +40,7 @@
     chip = s // 2
     partner = i + 1 - 2 * odd
     ahead = lax.rem(i + 2 - 4 * odd + n_space, n_space)
+    behind = lax.rem(i - 2 + 4 * odd + n_space, n_space)
     mate = s + 1 - 2 * core
 
     def peer(o):
@@ -50,22 +51,16 @@
 
     barrier = pltpu.get_barrier_semaphore()
 
-    def greet(d, carry):
-        pl.semaphore_signal(
-            barrier, inc=1, device_id={"space": lax.rem(i + d, n_space)},
-            device_id_type=pl.DeviceIdType.MESH,
-        )
-        return carry
-
-    lax.fori_loop(1, n_space, greet, 0)
-    pl.semaphore_signal(
-        barrier, inc=1, device_id={"snap": mate}, device_id_type=pl.DeviceIdType.MESH
-    )
-    for o in range(1, chips):
-        pl.semaphore_signal(
-            barrier, inc=1, device_id={"snap": peer(o)}, device_id_type=pl.DeviceIdType.MESH
-        )
-    pl.semaphore_wait(barrier, n_space - 1 + chips)
+    def signal(sem, **where):
+        pl.semaphore_signal(sem, inc=1, device_id=where, device_id_type=pl.DeviceIdType.MESH)
+
+    signal(barrier, space=partner)
+    signal(barrier, space=ahead)
+    signal(barrier, space=behind)
+    signal(barrier, snap=mate)
+    for o in range(1, chips):
+        signal(barrier, snap=peer(o))
+    pl.semaphore_wait(barrier, 3 + chips)
 
     def rows(t):
         return pl.ds(pl.multiple_of(t * ROWS, ROWS), ROWS)
@@ -151,6 +146,10 @@
 
     lax.fori_loop(0, chunks, launch, 0)
 
+    rounds = n_space // 4 - 1
+    signal(ring.at[0, 0], space=ahead)
+    signal(ring.at[0, 1], space=behind)
+
     for j in range(cells // 128):
         line = pl.ds(j, 1)
         weight = 0.5 * jnp.sqrt(volume_ref[line, :] * mask_ref[0, j].astype(jnp.float32))
@@ -218,7 +217,16 @@
         lax.fori_loop(h * per_block, (h + 1) * per_block, await_f, 0)
         product(f_origin(o), h)
 
-    lax.fori_loop(0, chunks + 1, step, 0)
+    lax.fori_loop(0, chunks // 2, step, 0)
+    for n in range(rounds):
+        pl.semaphore_wait(ring.at[n, 0], 1)
+        pl.semaphore_wait(ring.at[n, 1], 1)
+        if n < rounds - 1:
+            signal(ring.at[n + 1, 0], space=ahead)
+            signal(ring.at[n + 1, 1], space=behind)
+    signal(pair, space=partner)
+    lax.fori_loop(chunks // 2, chunks + 1, step, 0)
+    pl.semaphore_wait(pair, 1)
     for h in range(per_dev):
         product(s, h)
     lax.fori_loop(0, chunks, await_m, 0)
@@ -291,6 +299,7 @@
             dma((far, chunks, 3)), dma((far, chunks, 3)),
             dma((far, chunks, 3)), dma((far, chunks, 3)),
             dma((n_space,)), dma((n_space,)),
+            pltpu.SemaphoreType.REGULAR((n_space // 4 - 1, 2)), pltpu.SemaphoreType.REGULAR,
         ],
         compiler_params=pltpu.CompilerParams(
             collective_id=0, has_side_effects=True, vmem_limit_bytes=48 * 1024 * 1024

time: 43.8 us -> 44.1 us (level)
  no operation moved by 1% of the time
where the time goes in v3:
time: 44.1 us; the launch traced here: 44 us
  Pallas kernels  41.4 us (94%)
  local copies, waits for them, and re-layouts  2.54 us (6%)
    pallas_call x1, Pallas kernels, shards(): pl.pallas_call(functools.partial(kernel, n_space, n_snap), out_shape=jax....  41.4 us
    unnamed x8, local copies, waits for them, and re-layouts  2.54 us

profile of v3, /device:TPU:7, one launch (start us, length us, event | category | flops | bytes accessed | tf_op | source)
XLA Modules:
  0.0 44.0 jit_solution(8623570430848184882)
XLA Ops:
  0.0 0.0 copy-start
  0.0 0.0 copy-start.1
  0.0 1.3 %copy.7 = bf16[16,8,24,128]{3,1,2,0:T(8,128)(2,1)S(1)} copy(bf16[16,8,24,128]{3,2,1,0:T(8,128)(2,1)} %bitcast.12) | data formatting | bytes 1572864
  1.3 0.0 copy-start.2
  1.3 0.0 copy-done
  1.3 0.0 copy-done.1
  1.3 0.6 %copy-done.2 = s32[1,8]{1,0:T(1,128)S(1)} copy-done((s32[1,8]{1,0:T(1,128)S(1)}, s32[1,8]{1,0:T(1,128)}, u32[]{:S(2)}) %copy-start.2) | copy-done | bytes 56
  2.0 41.4 %shard_map.46 = f32[64,128]{1,0:T(8,128)S(1)} custom-call(bf16[128,3072]{1,0:T(8,128)(2,1)S(1)} %bitcast.8, f32[9,8,128]{2,1,0:T(8,128)S(1)} %bitcast.10, f32[8,128]{1,0:T(8,128)S(1)} %bitcast.11, s32[1,8]{1,0:T(1,128)S(1)} %copy-done.2), custom_call_target="tpu_custom_call" | custom-call | tf_op jit(solution)/shard_map/pallas_call | solution.py:284
  43.4 0.6 %copy.9 = f32[128,64]{0,1:T(8,128)} copy(f32[128,64]{0,1:T(8,128)S(1)} %bitcast.9) | data formatting | bytes 65536
Async XLA Ops:
  0.0 1.3 %copy-start = (f32[9,1,8,128]{3,2,1,0:T(8,128)S(1)}, f32[9,1,8,128]{3,2,1,0:T(8,128)}, u32[]{:S(2)}) copy-start(f32[9,1,8,128]{3,2,1,0:T(8,128)} %param.5) | copy-start | bytes 110596
  0.0 1.3 %copy-start.1 = (f32[1,8,128]{2,1,0:T(8,128)S(1)}, f32[1,8,128]{2,1,0:T(8,128)}, u32[]{:S(2)}) copy-start(f32[1,8,128]{2,1,0:T(8,128)} %param.6) | copy-start | bytes 12292
  1.3 0.7 %copy-start.2 = (s32[1,8]{1,0:T(1,128)S(1)}, s32[1,8]{1,0:T(1,128)}, u32[]{:S(2)}) copy-start(s32[1,8]{1,0:T(1,128)} %mask_ref.1) | copy-start | bytes 100

commit v4 on v2

--- a/solution.py
+++ b/solution.py
@@ -8,6 +8,7 @@
 from jax.sharding import PartitionSpec as P
 
 ROWS = 16
+PIECE = 32
 
 
 def remote(src, dst, send_sem, recv_sem, **where):
@@ -24,7 +25,7 @@
 def kernel(
     n_space, n_snap, u_ref, metric_ref, volume_ref, mask_ref, out_ref,
     coef_ref, side, far, gathered, partial, landed,
-    x_s, x_r, z_s, z_r, m_s, m_r, y_s, y_r, f_s, f_r, r_s, r_r,
+    x_s, x_r, z_s, z_r, m_s, m_r, y_s, y_r, f_s, f_r, r_s, r_r, flags, mask_sem,
 ):
     snaps, width = u_ref.shape
     cells = width // 3
@@ -48,6 +49,8 @@
     def origin(o):
         return 2 * lax.rem(chip + chips - o, chips) + core
 
+    mask_copy = pltpu.make_async_copy(mask_ref, flags, mask_sem)
+    mask_copy.start()
     barrier = pltpu.get_barrier_semaphore()
 
     def greet(d, carry):
@@ -151,9 +154,10 @@
 
     lax.fori_loop(0, chunks, launch, 0)
 
+    mask_copy.wait()
     for j in range(cells // 128):
         line = pl.ds(j, 1)
-        weight = 0.5 * jnp.sqrt(volume_ref[line, :] * mask_ref[0, j].astype(jnp.float32))
+        weight = 0.5 * jnp.sqrt(volume_ref[line, :] * flags[0, j].astype(jnp.float32))
         coef_ref[:, pl.ds(j * 128, 128)] = metric_ref[:, j, :] * weight
 
     def step(t, carry):
@@ -182,68 +186,74 @@
 
         return carry
 
-    def r_copy(block):
+    def r_copy(block, q):
+        piece = pl.ds(q * PIECE, PIECE)
         return remote(
-            partial.at[block], landed.at[i], r_s.at[block], r_r.at[i], space=block
-        )
-
-    def r_arrival(source):
+            partial.at[block, piece], landed.at[i, piece],
+            r_s.at[block, q], r_r.at[i, q], space=block,
+        )
+
+    def r_arrival(source, q):
+        piece = pl.ds(q * PIECE, PIECE)
         return remote(
-            partial.at[i], landed.at[source], r_s.at[source], r_r.at[source], space=source
-        )
-
-    def product(dev, h):
-        block = dev * per_dev + h
-        partial[block] = lax.dot_general(
-            gathered[dev, pl.ds(h * cols, cols), :], gathered[s], (((1,), (1,)), ((), ())),
+            partial.at[i, piece], landed.at[source, piece],
+            r_s.at[source, q], r_r.at[source, q], space=source,
+        )
+
+    per_block = cols // PIECE
+    per_piece = PIECE // ROWS
+    pieces = snaps // PIECE
+
+    def product(dev, n):
+        block = dev * per_dev + n // per_block
+        q = n % per_block
+        partial[block, pl.ds(q * PIECE, PIECE)] = lax.dot_general(
+            gathered[dev, pl.ds(n * PIECE, PIECE), :], gathered[s], (((1,), (1,)), ((), ())),
             preferred_element_type=jnp.float32,
         )
 
         @pl.when(block != i)
         def _():
-            r_copy(block).start()
+            r_copy(block, q).start()
 
     def await_m(t, carry):
         m_arrival(t).wait_recv()
         return carry
 
-    per_block = cols // ROWS
-
-    def product_f(o, h):
+    def product_f(o, n):
         def await_f(t, carry):
             for p in range(3):
                 f_arrival(o, t, p).wait_recv()
             return carry
 
-        lax.fori_loop(h * per_block, (h + 1) * per_block, await_f, 0)
-        product(f_origin(o), h)
+        lax.fori_loop(n * per_piece, (n + 1) * per_piece, await_f, 0)
+        product(f_origin(o), n)
 
     lax.fori_loop(0, chunks + 1, step, 0)
-    for h in range(per_dev):
-        product(s, h)
+    for n in range(pieces):
+        product(s, n)
     lax.fori_loop(0, chunks, await_m, 0)
-    for h in range(per_dev):
-        product(mate, h)
+    for n in range(pieces):
+        product(mate, n)
     lax.fori_loop(chunks + 1, chunks + 2, step, 0)
     for o in range(1, chips):
-        for h in range(per_dev - 1):
-            product(origin(o), h)
+        for n in range(pieces - 1):
+            product(origin(o), n)
+        for n in range(pieces - 1):
+            product_f(o, n)
     lax.fori_loop(chunks + 2, chunks + 3, step, 0)
     for o in range(1, chips):
-        for h in range(per_dev - 1):
-            product_f(o, h)
+        product(origin(o), pieces - 1)
     for o in range(1, chips):
-        product(origin(o), per_dev - 1)
-    for o in range(1, chips):
-        product_f(o, per_dev - 1)
+        product_f(o, pieces - 1)
 
     def add(d, total):
         source = lax.rem(i + d, n_space)
-        r_arrival(source).wait_recv()
+        for q in range(per_block):
+            r_arrival(source, q).wait_recv()
         return total + landed[source]
 
-    total = lax.fori_loop(1, n_space, add, partial[i])
-    out_ref[...] = total
+    out_ref[...] = lax.fori_loop(1, n_space, add, partial[i])
 
     def drain(t, carry):
         m_copy(t).wait_send()
@@ -258,7 +268,8 @@
     lax.fori_loop(0, chunks, drain, 0)
 
     def drain_r(d, carry):
-        r_copy(lax.rem(i + d, n_space)).wait_send()
+        for q in range(per_block):
+            r_copy(lax.rem(i + d, n_space), q).wait_send()
         return carry
 
     lax.fori_loop(1, n_space, drain_r, 0)
@@ -277,7 +288,7 @@
         functools.partial(kernel, n_space, n_snap),
         out_shape=jax.ShapeDtypeStruct((cols, snaps), jnp.float32),
         in_specs=[pl.BlockSpec(memory_space=pltpu.VMEM)] * 3
-        + [pl.BlockSpec(memory_space=pltpu.SMEM)],
+        + [pl.BlockSpec(memory_space=pltpu.HBM)],
         out_specs=pl.BlockSpec(memory_space=pltpu.VMEM),
         scratch_shapes=[
             pltpu.VMEM((9, width // 3), jnp.float32),
@@ -290,7 +301,8 @@
             dma((chunks,)), dma((chunks,)),
             dma((far, chunks, 3)), dma((far, chunks, 3)),
             dma((far, chunks, 3)), dma((far, chunks, 3)),
-            dma((n_space,)), dma((n_space,)),
+            dma((n_space, cols // PIECE)), dma((n_space, cols // PIECE)),
+            pltpu.SMEM(blade_mask.shape, jnp.int32), dma,
         ],
         compiler_params=pltpu.CompilerParams(
             collective_id=0, has_side_effects=True, vmem_limit_bytes=48 * 1024 * 1024

time: 43.8 us -> 45.3 us (1.034)
  Pallas kernels: 41.1 us -> 42.6 us
    pallas_call x1, Pallas kernels: 41.1 us -> 42.6 us  [shards(): pl.pallas_call(functools.partial(kernel, n_space, n_snap), out_shape=jax....]
where the time goes in v4:
time: 45.3 us; the launch traced here: 45.2 us
  Pallas kernels  42.6 us (94%)
  local copies, waits for them, and re-layouts  2.54 us (6%)
    pallas_call x1, Pallas kernels, shards(): pl.pallas_call(functools.partial(kernel, n_space, n_snap), out_shape=jax....  42.6 us
    unnamed x8, local copies, waits for them, and re-layouts  2.54 us

profile of v4, /device:TPU:7, one launch (start us, length us, event | category | flops | bytes accessed | tf_op | source)
XLA Modules:
  0.0 45.2 jit_solution(8931152795590986680)
XLA Ops:
  0.0 0.0 copy-start
  0.0 0.0 copy-start.1
  0.0 1.3 %copy.7 = bf16[16,8,24,128]{3,1,2,0:T(8,128)(2,1)S(1)} copy(bf16[16,8,24,128]{3,2,1,0:T(8,128)(2,1)} %bitcast.12) | data formatting | bytes 1572864
  1.3 0.0 copy-start.2
  1.3 0.0 copy-done
  1.3 0.0 copy-done.1
  1.3 0.6 %copy-done.2 = s32[1,8]{1,0:T(1,128)S(1)} copy-done((s32[1,8]{1,0:T(1,128)S(1)}, s32[1,8]{1,0:T(1,128)}, u32[]{:S(2)}) %copy-start.2) | copy-done | bytes 56
  2.0 42.6 %shard_map.46 = f32[64,128]{1,0:T(8,128)S(1)} custom-call(bf16[128,3072]{1,0:T(8,128)(2,1)S(1)} %bitcast.8, f32[9,8,128]{2,1,0:T(8,128)S(1)} %bitcast.10, f32[8,128]{1,0:T(8,128)S(1)} %bitcast.11, s32[1,8]{1,0:T(1,128)S(1)} %copy-done.2), custom_call_target="tpu_custom_call" | custom-call | tf_op jit(solution)/shard_map/pallas_call | solution.py:287
  44.6 0.6 %copy.9 = f32[128,64]{0,1:T(8,128)} copy(f32[128,64]{0,1:T(8,128)S(1)} %bitcast.9) | data formatting | bytes 65536
Async XLA Ops:
  0.0 1.3 %copy-start = (f32[9,1,8,128]{3,2,1,0:T(8,128)S(1)}, f32[9,1,8,128]{3,2,1,0:T(8,128)}, u32[]{:S(2)}) copy-start(f32[9,1,8,128]{3,2,1,0:T(8,128)} %param.5) | copy-start | bytes 110596
  0.0 1.3 %copy-start.1 = (f32[1,8,128]{2,1,0:T(8,128)S(1)}, f32[1,8,128]{2,1,0:T(8,128)}, u32[]{:S(2)}) copy-start(f32[1,8,128]{2,1,0:T(8,128)} %param.6) | copy-start | bytes 12292
  1.3 0.7 %copy-start.2 = (s32[1,8]{1,0:T(1,128)S(1)}, s32[1,8]{1,0:T(1,128)}, u32[]{:S(2)}) copy-start(s32[1,8]{1,0:T(1,128)} %mask_ref.1) | copy-start | bytes 100

commit v5 on v2

--- a/solution.py
+++ b/solution.py
@@ -8,6 +8,8 @@
 from jax.sharding import PartitionSpec as P
 
 ROWS = 16
+Z_LAG = 2
+Y_LAG = 4
 
 
 def remote(src, dst, send_sem, recv_sem, **where):
@@ -24,7 +26,7 @@
 def kernel(
     n_space, n_snap, u_ref, metric_ref, volume_ref, mask_ref, out_ref,
     coef_ref, side, far, gathered, partial, landed,
-    x_s, x_r, z_s, z_r, m_s, m_r, y_s, y_r, f_s, f_r, r_s, r_r,
+    x_s, x_r, z_s, z_r, m_s, m_r, y_s, y_r, f_s, f_r, r_s, r_r, flags, mask_sem,
 ):
     snaps, width = u_ref.shape
     cells = width // 3
@@ -48,6 +50,8 @@
     def origin(o):
         return 2 * lax.rem(chip + chips - o, chips) + core
 
+    mask_copy = pltpu.make_async_copy(mask_ref, flags, mask_sem)
+    mask_copy.start()
     barrier = pltpu.get_barrier_semaphore()
 
     def greet(d, carry):
@@ -151,9 +155,10 @@
 
     lax.fori_loop(0, chunks, launch, 0)
 
+    mask_copy.wait()
     for j in range(cells // 128):
         line = pl.ds(j, 1)
-        weight = 0.5 * jnp.sqrt(volume_ref[line, :] * mask_ref[0, j].astype(jnp.float32))
+        weight = 0.5 * jnp.sqrt(volume_ref[line, :] * flags[0, j].astype(jnp.float32))
         coef_ref[:, pl.ds(j * 128, 128)] = metric_ref[:, j, :] * weight
 
     def step(t, carry):
@@ -163,22 +168,22 @@
                 x_copy(t, p).wait_recv()
                 z_copy(t, p).start()
 
-        @pl.when(jnp.logical_and(t >= 1, t < chunks + 1))
+        @pl.when(jnp.logical_and(t >= Z_LAG, t < chunks + Z_LAG))
         def _():
             for p in range(3):
-                z_copy(t - 1, p).wait_recv()
-            vorticity(t - 1)
+                z_copy(t - Z_LAG, p).wait_recv()
+            vorticity(t - Z_LAG)
             for p in range(3):
                 for o in range(1, chips):
-                    y_copy(o, t - 1, p).start()
-            m_copy(t - 1).start()
-
-        @pl.when(t >= 3)
+                    y_copy(o, t - Z_LAG, p).start()
+            m_copy(t - Z_LAG).start()
+
+        @pl.when(t >= Y_LAG)
         def _():
             for p in range(3):
                 for o in range(1, chips):
-                    y_arrival(o, t - 3, p).wait_recv()
-                    f_copy(o, t - 3, p).start()
+                    y_arrival(o, t - Y_LAG, p).wait_recv()
+                    f_copy(o, t - Y_LAG, p).start()
 
         return carry
 
@@ -218,17 +223,29 @@
         lax.fori_loop(h * per_block, (h + 1) * per_block, await_f, 0)
         product(f_origin(o), h)
 
-    lax.fori_loop(0, chunks + 1, step, 0)
-    for h in range(per_dev):
-        product(s, h)
+    def whole_product(dev):
+        result = lax.dot_general(
+            gathered[dev], gathered[s], (((1,), (1,)), ((), ())),
+            preferred_element_type=jnp.float32,
+        )
+        for h in range(per_dev):
+            block = dev * per_dev + h
+            partial[block] = result[h * cols:(h + 1) * cols]
+
+            @pl.when(block != i)
+            def _():
+                r_copy(block).start()
+
+    done = chunks + Z_LAG
+    lax.fori_loop(0, done, step, 0)
+    whole_product(s)
     lax.fori_loop(0, chunks, await_m, 0)
-    for h in range(per_dev):
-        product(mate, h)
-    lax.fori_loop(chunks + 1, chunks + 2, step, 0)
+    whole_product(mate)
+    lax.fori_loop(done, chunks + Y_LAG - 1, step, 0)
     for o in range(1, chips):
         for h in range(per_dev - 1):
             product(origin(o), h)
-    lax.fori_loop(chunks + 2, chunks + 3, step, 0)
+    lax.fori_loop(chunks + Y_LAG - 1, chunks + Y_LAG, step, 0)
     for o in range(1, chips):
         for h in range(per_dev - 1):
             product_f(o, h)
@@ -277,7 +294,7 @@
         functools.partial(kernel, n_space, n_snap),
         out_shape=jax.ShapeDtypeStruct((cols, snaps), jnp.float32),
         in_specs=[pl.BlockSpec(memory_space=pltpu.VMEM)] * 3
-        + [pl.BlockSpec(memory_space=pltpu.SMEM)],
+        + [pl.BlockSpec(memory_space=pltpu.HBM)],
         out_specs=pl.BlockSpec(memory_space=pltpu.VMEM),
         scratch_shapes=[
             pltpu.VMEM((9, width // 3), jnp.float32),
@@ -291,6 +308,7 @@
             dma((far, chunks, 3)), dma((far, chunks, 3)),
             dma((far, chunks, 3)), dma((far, chunks, 3)),
             dma((n_space,)), dma((n_space,)),
+            pltpu.SMEM(blade_mask.shape, jnp.int32), dma,
         ],
         compiler_params=pltpu.CompilerParams(
             collective_id=0, has_side_effects=True, vmem_limit_bytes=48 * 1024 * 1024

time: 43.8 us -> 41.4 us (0.945)
  Pallas kernels: 41.1 us -> 38.7 us
    pallas_call x1, Pallas kernels: 41.1 us -> 38.7 us  [shards(): pl.pallas_call(functools.partial(kernel, n_space, n_snap), out_shape=jax....]
where the time goes in v5:
time: 41.4 us; the launch traced here: 41.3 us
  Pallas kernels  38.7 us (93%)
  local copies, waits for them, and re-layouts  2.54 us (6%)
    pallas_call x1, Pallas kernels, shards(): pl.pallas_call(functools.partial(kernel, n_space, n_snap), out_shape=jax....  38.7 us
    unnamed x8, local copies, waits for them, and re-layouts  2.54 us

profile of v5, /device:TPU:7, one launch (start us, length us, event | category | flops | bytes accessed | tf_op | source)
XLA Modules:
  0.0 41.3 jit_solution(9899670696997068670)
XLA Ops:
  0.0 0.0 copy-start
  0.0 0.0 copy-start.1
  0.0 1.3 %copy.7 = bf16[16,8,24,128]{3,1,2,0:T(8,128)(2,1)S(1)} copy(bf16[16,8,24,128]{3,2,1,0:T(8,128)(2,1)} %bitcast.12) | data formatting | bytes 1572864
  1.3 0.0 copy-start.2
  1.3 0.0 copy-done
  1.3 0.0 copy-done.1
  1.3 0.6 %copy-done.2 = s32[1,8]{1,0:T(1,128)S(1)} copy-done((s32[1,8]{1,0:T(1,128)S(1)}, s32[1,8]{1,0:T(1,128)}, u32[]{:S(2)}) %copy-start.2) | copy-done | bytes 56
  2.0 38.7 %shard_map.46 = f32[64,128]{1,0:T(8,128)S(1)} custom-call(bf16[128,3072]{1,0:T(8,128)(2,1)S(1)} %bitcast.8, f32[9,8,128]{2,1,0:T(8,128)S(1)} %bitcast.10, f32[8,128]{1,0:T(8,128)S(1)} %bitcast.11, s32[1,8]{1,0:T(1,128)S(1)} %copy-done.2), custom_call_target="tpu_custom_call" | custom-call | tf_op jit(solution)/shard_map/pallas_call | solution.py:293
  40.6 0.6 %copy.9 = f32[128,64]{0,1:T(8,128)} copy(f32[128,64]{0,1:T(8,128)S(1)} %bitcast.9) | data formatting | bytes 65536
Async XLA Ops:
  0.0 1.3 %copy-start = (f32[9,1,8,128]{3,2,1,0:T(8,128)S(1)}, f32[9,1,8,128]{3,2,1,0:T(8,128)}, u32[]{:S(2)}) copy-start(f32[9,1,8,128]{3,2,1,0:T(8,128)} %param.5) | copy-start | bytes 110596
  0.0 1.3 %copy-start.1 = (f32[1,8,128]{2,1,0:T(8,128)S(1)}, f32[1,8,128]{2,1,0:T(8,128)}, u32[]{:S(2)}) copy-start(f32[1,8,128]{2,1,0:T(8,128)} %param.6) | copy-start | bytes 12292
  1.3 0.7 %copy-start.2 = (s32[1,8]{1,0:T(1,128)S(1)}, s32[1,8]{1,0:T(1,128)}, u32[]{:S(2)}) copy-start(s32[1,8]{1,0:T(1,128)} %mask_ref.1) | copy-start | bytes 100

commit v6 on v5

--- a/solution.py
+++ b/solution.py
@@ -26,7 +26,7 @@
 def kernel(
     n_space, n_snap, u_ref, metric_ref, volume_ref, mask_ref, out_ref,
     coef_ref, side, far, gathered, partial, landed,
-    x_s, x_r, z_s, z_r, m_s, m_r, y_s, y_r, f_s, f_r, r_s, r_r, flags, mask_sem,
+    x_s, x_r, z_s, z_r, m_s, m_r, y_s, y_r, f_s, f_r, r_s, r_r, flags, mask_sem, ring, pair,
 ):
     snaps, width = u_ref.shape
     cells = width // 3
@@ -42,6 +42,7 @@
     chip = s // 2
     partner = i + 1 - 2 * odd
     ahead = lax.rem(i + 2 - 4 * odd + n_space, n_space)
+    behind = lax.rem(i - 2 + 4 * odd + n_space, n_space)
     mate = s + 1 - 2 * core
 
     def peer(o):
@@ -54,22 +55,16 @@
     mask_copy.start()
     barrier = pltpu.get_barrier_semaphore()
 
-    def greet(d, carry):
-        pl.semaphore_signal(
-            barrier, inc=1, device_id={"space": lax.rem(i + d, n_space)},
-            device_id_type=pl.DeviceIdType.MESH,
-        )
-        return carry
-
-    lax.fori_loop(1, n_space, greet, 0)
-    pl.semaphore_signal(
-        barrier, inc=1, device_id={"snap": mate}, device_id_type=pl.DeviceIdType.MESH
-    )
-    for o in range(1, chips):
-        pl.semaphore_signal(
-            barrier, inc=1, device_id={"snap": peer(o)}, device_id_type=pl.DeviceIdType.MESH
-        )
-    pl.semaphore_wait(barrier, n_space - 1 + chips)
+    def signal(sem, **where):
+        pl.semaphore_signal(sem, inc=1, device_id=where, device_id_type=pl.DeviceIdType.MESH)
+
+    signal(barrier, space=partner)
+    signal(barrier, space=ahead)
+    signal(barrier, space=behind)
+    signal(barrier, snap=mate)
+    for o in range(1, chips):
+        signal(barrier, snap=peer(o))
+    pl.semaphore_wait(barrier, 3 + chips)
 
     def rows(t):
         return pl.ds(pl.multiple_of(t * ROWS, ROWS), ROWS)
@@ -155,6 +150,9 @@
 
     lax.fori_loop(0, chunks, launch, 0)
 
+    rounds = n_space // 4 - 1
+    signal(ring.at[0, 0], space=ahead)
+    signal(ring.at[0, 1], space=behind)
     mask_copy.wait()
     for j in range(cells // 128):
         line = pl.ds(j, 1)
@@ -162,11 +160,14 @@
         coef_ref[:, pl.ds(j * 128, 128)] = metric_ref[:, j, :] * weight
 
     def step(t, carry):
-        @pl.when(t < chunks)
-        def _():
-            for p in range(3):
-                x_copy(t, p).wait_recv()
-                z_copy(t, p).start()
+        def forward(parts):
+            @pl.when(t < chunks)
+            def _():
+                for p in parts:
+                    x_copy(t, p).wait_recv()
+                    z_copy(t, p).start()
+
+        forward(range(2))
 
         @pl.when(jnp.logical_and(t >= Z_LAG, t < chunks + Z_LAG))
         def _():
@@ -178,6 +179,8 @@
                     y_copy(o, t - Z_LAG, p).start()
             m_copy(t - Z_LAG).start()
 
+        forward(range(2, 3))
+
         @pl.when(t >= Y_LAG)
         def _():
             for p in range(3):
@@ -237,7 +240,16 @@
                 r_copy(block).start()
 
     done = chunks + Z_LAG
-    lax.fori_loop(0, done, step, 0)
+    lax.fori_loop(0, chunks // 2, step, 0)
+    for n in range(rounds):
+        pl.semaphore_wait(ring.at[n, 0], 1)
+        pl.semaphore_wait(ring.at[n, 1], 1)
+        if n < rounds - 1:
+            signal(ring.at[n + 1, 0], space=ahead)
+            signal(ring.at[n + 1, 1], space=behind)
+    signal(pair, space=partner)
+    lax.fori_loop(chunks // 2, done, step, 0)
+    pl.semaphore_wait(pair, 1)
     whole_product(s)
     lax.fori_loop(0, chunks, await_m, 0)
     whole_product(mate)
@@ -309,6 +321,7 @@
             dma((far, chunks, 3)), dma((far, chunks, 3)),
             dma((n_space,)), dma((n_space,)),
             pltpu.SMEM(blade_mask.shape, jnp.int32), dma,
+            pltpu.SemaphoreType.REGULAR((n_space // 4 - 1, 2)), pltpu.SemaphoreType.REGULAR,
         ],
         compiler_params=pltpu.CompilerParams(
             collective_id=0, has_side_effects=True, vmem_limit_bytes=48 * 1024 * 1024

time: 41.4 us -> 41 us (level)
  no operation moved by 1% of the time
where the time goes in v6:
time: 41 us; the launch traced here: 40.9 us
  Pallas kernels  38.3 us (93%)
  local copies, waits for them, and re-layouts  2.54 us (6%)
    pallas_call x1, Pallas kernels, shards(): pl.pallas_call(functools.partial(kernel, n_space, n_snap), out_shape=jax....  38.3 us
    unnamed x8, local copies, waits for them, and re-layouts  2.54 us

profile of v6, /device:TPU:7, one launch (start us, length us, event | category | flops | bytes accessed | tf_op | source)
XLA Modules:
  0.0 40.9 jit_solution(14087335642317036262)
XLA Ops:
  0.0 0.0 copy-start
  0.0 0.0 copy-start.1
  0.0 1.3 %copy.7 = bf16[16,8,24,128]{3,1,2,0:T(8,128)(2,1)S(1)} copy(bf16[16,8,24,128]{3,2,1,0:T(8,128)(2,1)} %bitcast.12) | data formatting | bytes 1572864
  1.3 0.0 copy-start.2
  1.3 0.0 copy-done
  1.3 0.0 copy-done.1
  1.3 0.6 %copy-done.2 = s32[1,8]{1,0:T(1,128)S(1)} copy-done((s32[1,8]{1,0:T(1,128)S(1)}, s32[1,8]{1,0:T(1,128)}, u32[]{:S(2)}) %copy-start.2) | copy-done | bytes 56
  2.0 38.3 %shard_map.46 = f32[64,128]{1,0:T(8,128)S(1)} custom-call(bf16[128,3072]{1,0:T(8,128)(2,1)S(1)} %bitcast.8, f32[9,8,128]{2,1,0:T(8,128)S(1)} %bitcast.10, f32[8,128]{1,0:T(8,128)S(1)} %bitcast.11, s32[1,8]{1,0:T(1,128)S(1)} %copy-done.2), custom_call_target="tpu_custom_call" | custom-call | tf_op jit(solution)/shard_map/pallas_call | solution.py:305
  40.3 0.6 %copy.9 = f32[128,64]{0,1:T(8,128)} copy(f32[128,64]{0,1:T(8,128)S(1)} %bitcast.9) | data formatting | bytes 65536
Async XLA Ops:
  0.0 1.3 %copy-start = (f32[9,1,8,128]{3,2,1,0:T(8,128)S(1)}, f32[9,1,8,128]{3,2,1,0:T(8,128)}, u32[]{:S(2)}) copy-start(f32[9,1,8,128]{3,2,1,0:T(8,128)} %param.5) | copy-start | bytes 110596
  0.0 1.3 %copy-start.1 = (f32[1,8,128]{2,1,0:T(8,128)S(1)}, f32[1,8,128]{2,1,0:T(8,128)}, u32[]{:S(2)}) copy-start(f32[1,8,128]{2,1,0:T(8,128)} %param.6) | copy-start | bytes 12292
  1.3 0.7 %copy-start.2 = (s32[1,8]{1,0:T(1,128)S(1)}, s32[1,8]{1,0:T(1,128)}, u32[]{:S(2)}) copy-start(s32[1,8]{1,0:T(1,128)} %mask_ref.1) | copy-start | bytes 100

commit v7 on v6

--- a/solution.py
+++ b/solution.py
@@ -257,10 +257,10 @@
     for o in range(1, chips):
         for h in range(per_dev - 1):
             product(origin(o), h)
-    lax.fori_loop(chunks + Y_LAG - 1, chunks + Y_LAG, step, 0)
     for o in range(1, chips):
         for h in range(per_dev - 1):
             product_f(o, h)
+    lax.fori_loop(chunks + Y_LAG - 1, chunks + Y_LAG, step, 0)
     for o in range(1, chips):
         product(origin(o), per_dev - 1)
     for o in range(1, chips):

time: 41 us -> 41.1 us (level)
  no operation moved by 1% of the time
where the time goes in v7:
time: 41.1 us; the launch traced here: 40.9 us
  Pallas kernels  38.3 us (93%)
  local copies, waits for them, and re-layouts  2.54 us (6%)
    pallas_call x1, Pallas kernels, shards(): pl.pallas_call(functools.partial(kernel, n_space, n_snap), out_shape=jax....  38.3 us
    unnamed x8, local copies, waits for them, and re-layouts  2.54 us

profile of v7, /device:TPU:7, one launch (start us, length us, event | category | flops | bytes accessed | tf_op | source)
XLA Modules:
  0.0 40.9 jit_solution(10284696647829323669)
XLA Ops:
  0.0 0.0 copy-start
  0.0 0.0 copy-start.1
  0.0 1.3 %copy.7 = bf16[16,8,24,128]{3,1,2,0:T(8,128)(2,1)S(1)} copy(bf16[16,8,24,128]{3,2,1,0:T(8,128)(2,1)} %bitcast.12) | data formatting | bytes 1572864
  1.3 0.0 copy-start.2
  1.3 0.0 copy-done
  1.3 0.0 copy-done.1
  1.3 0.6 %copy-done.2 = s32[1,8]{1,0:T(1,128)S(1)} copy-done((s32[1,8]{1,0:T(1,128)S(1)}, s32[1,8]{1,0:T(1,128)}, u32[]{:S(2)}) %copy-start.2) | copy-done | bytes 56
  2.0 38.3 %shard_map.46 = f32[64,128]{1,0:T(8,128)S(1)} custom-call(bf16[128,3072]{1,0:T(8,128)(2,1)S(1)} %bitcast.8, f32[9,8,128]{2,1,0:T(8,128)S(1)} %bitcast.10, f32[8,128]{1,0:T(8,128)S(1)} %bitcast.11, s32[1,8]{1,0:T(1,128)S(1)} %copy-done.2), custom_call_target="tpu_custom_call" | custom-call | tf_op jit(solution)/shard_map/pallas_call | solution.py:305
  40.3 0.6 %copy.9 = f32[128,64]{0,1:T(8,128)} copy(f32[128,64]{0,1:T(8,128)S(1)} %bitcast.9) | data formatting | bytes 65536
Async XLA Ops:
  0.0 1.3 %copy-start = (f32[9,1,8,128]{3,2,1,0:T(8,128)S(1)}, f32[9,1,8,128]{3,2,1,0:T(8,128)}, u32[]{:S(2)}) copy-start(f32[9,1,8,128]{3,2,1,0:T(8,128)} %param.5) | copy-start | bytes 110596
  0.0 1.3 %copy-start.1 = (f32[1,8,128]{2,1,0:T(8,128)S(1)}, f32[1,8,128]{2,1,0:T(8,128)}, u32[]{:S(2)}) copy-start(f32[1,8,128]{2,1,0:T(8,128)} %param.6) | copy-start | bytes 12292
  1.3 0.7 %copy-start.2 = (s32[1,8]{1,0:T(1,128)S(1)}, s32[1,8]{1,0:T(1,128)}, u32[]{:S(2)}) copy-start(s32[1,8]{1,0:T(1,128)} %mask_ref.1) | copy-start | bytes 100
